TPU v7x, 512 devices: a whole 4x4x16 slice. The times are simulated.
512 devices in a mesh: vel: 64 (over z, y), space: 8 (over x, core).
Axes of the slice: x: 4, y: 4, z: 16, core: 2. Of those that a mesh axis runs over, the one named last changes fastest.
Arguments:
- distribution: float32 [16384, 64, 128], P('vel', 'space'), may hold values from 0 to 11, as said below
- rate_class: int32 [64, 128], P('space'), may hold values from 0 to 7
- boundary_obstacle_indicator: int32 [64, 128], P('space'), may hold values 0 or 1
Outputs:
- field_out: float32 [16384, 64, 128], P('vel', 'space')
- latest_conserved_fields: float32 [5, 64, 128], P(None, 'space')
Inputs may be any that keep to these rules, and one draw needn't show every extreme that they name: `distribution`: every entry positive.
All inputs are finite; a program needn't handle non-finite values. No bound on the sum of `boundary_obstacle_indicator` on one device may be relied on, other than what follows from the above.
Results may differ from a plain program's by a relative error of at most 0.0003.
Values sent between devices are 32-bit elements; how exact they have to be, the bound alone decides.
No kernel may reach another device: no remote copies, remote signals or barrier semaphores. Data moves between devices by JAX's collectives and lax.ppermute only.
A program may use at most 64 MiB of HBM per device.

v0:
```python
import jax
import jax.numpy as jnp
import numpy as np
from jax import lax
from jax.experimental import pallas as pl
from jax.experimental.pallas import tpu as pltpu
from jax.sharding import PartitionSpec as P

VX, VY, VZ = 32, 32, 16
SWEEPS = 4
EDGE = 5.0
STEP = 0.1
HX = 2.0 * EDGE / VX
HY = 2.0 * EDGE / VY
HZ = 2.0 * EDGE / VZ
QUAD = float(HX * HY * HZ / (2.0 * np.pi) ** 1.5)
SPEED_X = [-EDGE + (i + 0.5) * HX for i in range(VX)]
SPEED_Y = [-EDGE + (i + 0.5) * HY for i in range(VY)]
SPEED_Z = [-EDGE + (i + 0.5) * HZ for i in range(VZ)]
F32 = jnp.float32

MOMENTS = [
    ((0, 0, 0),),
    ((1, 0, 0),),
    ((0, 1, 0),),
    ((0, 0, 1),),
    ((2, 0, 0), (0, 2, 0), (0, 0, 2)),
    ((2, 0, 0),),
    ((0, 2, 0),),
    ((1, 1, 0),),
    ((1, 0, 1),),
    ((0, 1, 1),),
    ((3, 0, 0), (1, 2, 0), (1, 0, 2)),
    ((2, 1, 0), (0, 3, 0), (0, 1, 2)),
    ((2, 0, 1), (0, 2, 1), (0, 0, 3)),
]


def times(moment, axis):
    return tuple(tuple(p + (d == axis) for d, p in enumerate(m)) for m in moment)


def key_of(moment):
    return tuple(sorted(moment))


PLAIN = []
for _m in MOMENTS + [times(m, 0) for m in MOMENTS] + [times(m, 1) for m in MOMENTS]:
    if key_of(_m) not in PLAIN:
        PLAIN.append(key_of(_m))
AT = {k: i for i, k in enumerate(PLAIN)}
ABS_X = len(PLAIN)
ABS_Y = ABS_X + 13
SETS = ABS_Y + 13
SLOTS = 64
FIRST_SET = 7


def slot_of(i):
    return FIRST_SET + i if i < 5 else FIRST_SET + 6 + i


def row_up(i):
    return (i // 8, i % 8) if i < 48 else (6, i - 48)


def row_down(i):
    return (12 + i // 8, i % 8) if i < 48 else (6, i - 45)


def rows_of():
    return lax.broadcasted_iota(jnp.int32, (8, 128), 0)


def added_up(terms):
    total = None
    for t in terms:
        total = t if total is None else total + t
    return total


def place():
    vel = lax.axis_index("vel")
    return lax.rem(vel, 4), lax.div(vel, 4)


def local_y(block, iy):
    return -EDGE + ((block * 8 + iy).astype(F32) + 0.5) * HY


def local_z(iz):
    return -EDGE + (iz.astype(F32) + 0.5) * HZ


def moved(value, ix, courant_y, shift, row, before, after):
    courant_x = STEP * abs(SPEED_X[ix])
    if SPEED_X[ix] > 0:
        beside = jnp.where(row == 0, before, pltpu.roll(value, 1, 0))
    else:
        beside = jnp.where(row == 7, after, pltpu.roll(value, 7, 0))
    along = pltpu.roll(value, shift, 1)
    return ((1.0 - courant_x) - courant_y) * value + courant_x * beside + courant_y * along


def powers():
    full = [(a, b) for a in range(5) for b in range(5 - a)]
    odd = [(a, b) for a in range(1, 5) for b in range(5 - a)]
    return {p: i for i, p in enumerate(full)}, {p: 15 + i for i, p in enumerate(odd)}


def moments_kernel(
    f_hbm, part_ref, to_next_ref, to_prev_ref, inner_last_ref, inner_first_ref,
    field, acc, edge_acc, sems,
):
    block, iz = place()
    row = rows_of()
    shift = jnp.where(block >= 2, 1, 127)
    full_at, odd_at = powers()

    def chunk(i):
        rows = pl.ds(i * 64, 64)
        return pltpu.make_async_copy(f_hbm.at[rows], field.at[rows], sems.at[i])

    for i in range(4):
        chunk(i).start()
    acc[...] = jnp.zeros_like(acc)
    edge_acc[...] = jnp.zeros_like(edge_acc)
    lane_x = (row.astype(F32) + 0.5) * HX

    def over_y(iy, carry):
        @pl.when(lax.rem(iy, 2) == 0)
        def _():
            chunk(lax.div(iy, 2)).wait()

        sy = local_y(block, iy)
        courant_y = STEP * jnp.abs(sy)
        sums = [[None] * 5, [None] * 5]
        for ix in range(VX):
            half = 1 if SPEED_X[ix] > 0 else 0
            k = ix % 16
            raw = field[iy * 32 + ix]
            at = (2 * iy + k // 8, slice(k % 8, k % 8 + 1), slice(None))
            if half:
                to_next_ref[at] = raw[7:8, :]
                inner_last_ref[at] = raw[6:7, :]
            else:
                to_prev_ref[at] = raw[0:1, :]
                inner_first_ref[at] = raw[1:2, :]
            value = moved(raw, ix, courant_y, shift, row, 0.0, 0.0)
            for a in range(5):
                term = value if a == 0 else (SPEED_X[ix] ** a) * value
                sums[half][a] = term if sums[half][a] is None else sums[half][a] + term
        power = [1.0, sy, sy * sy, sy * sy * sy, sy * sy * sy * sy]
        full = [sums[1][a] + sums[0][a] for a in range(5)]
        odd = [sums[1][a] - sums[0][a] for a in range(5)]
        for (a, b), n in full_at.items():
            acc[n] = acc[n] + power[b] * full[a]
        for (a, b), n in odd_at.items():
            acc[n] = acc[n] + power[b] * odd[a]
        for side, ref, base in ((0, to_next_ref, 0.0), (1, to_prev_ref, -EDGE)):
            edge = [None] * 5
            for j in range(2):
                sx = lane_x + (base + 8 * HX * j)
                term = (STEP * jnp.abs(sx)) * ref[2 * iy + j]
                for a in range(5):
                    term = term if a == 0 else sx * term
                    edge[a] = term if edge[a] is None else edge[a] + term
            for (a, b), n in full_at.items():
                edge_acc[side, n] = edge_acc[side, n] + power[b] * edge[a]
        return carry

    lax.fori_loop(0, 8, over_y, 0)
    sz = local_z(iz)
    zs = [QUAD * jnp.ones((), F32), QUAD * sz, QUAD * sz * sz, QUAD * sz * sz * sz]
    sign = jnp.where(block >= 2, 1.0, -1.0).astype(F32)
    zy = [sign * z for z in zs]

    def all_sets(full, odd):
        out = [added_up(zs[c] * full(a, b) for a, b, c in monos) for monos in PLAIN]
        out += [added_up(zs[c] * odd(a + 1, b) for a, b, c in monos) for monos in MOMENTS]
        out += [added_up(zy[c] * full(a, b + 1) for a, b, c in monos) for monos in MOMENTS]
        return out

    for i, v in enumerate(all_sets(lambda a, b: acc[full_at[a, b]], lambda a, b: acc[odd_at[a, b]])):
        part_ref[slot_of(i)] = v
    part_ref[6] = jnp.zeros((8, 128), F32)
    for side, where in ((0, row_up), (1, row_down)):
        lines = {p: jnp.sum(edge_acc[side, n], axis=0, keepdims=True) for p, n in full_at.items()}
        factor = -1.0 if side else 1.0
        for i, v in enumerate(
            all_sets(lambda a, b: lines[a, b], lambda a, b: factor * lines[a, b])
        ):
            slot, r = where(i)
            part_ref[slot, r : r + 1, :] = v


def diffuse(own_source, far_source, row):
    own, far = own_source, far_source
    for _ in range(SWEEPS):
        own_down, far_down = pltpu.roll(own, 1, 0), pltpu.roll(far, 1, 0)
        own_up, far_up = pltpu.roll(own, 7, 0), pltpu.roll(far, 7, 0)
        new_own = (
            jnp.where(row == 0, far_down, own_down)
            + jnp.where(row == 7, far_up, own_up)
            + pltpu.roll(own, 1, 1)
            + pltpu.roll(own, 127, 1)
        )
        new_far = (
            jnp.where(row == 0, own_down, far_down)
            + jnp.where(row == 7, own_up, far_up)
            + pltpu.roll(far, 1, 1)
            + pltpu.roll(far, 127, 1)
        )
        own = (own_source + new_own) * 0.2
        far = (far_source + new_far) * 0.2
    return own


def heat_flux(m):
    inv = 1.0 / m[0]
    u = [m[1] * inv, m[2] * inv, m[3] * inv]
    p_zz = m[4] - m[5] - m[6]
    p = [[m[5], m[7], m[8]], [m[7], m[6], m[9]], [m[8], m[9], p_zz]]
    sq = u[0] * u[0] + u[1] * u[1] + u[2] * u[2]
    mass_sq = 2.0 * m[0] * sq
    return [
        0.5
        * (
            m[10 + i]
            - 2.0 * (u[0] * p[i][0] + u[1] * p[i][1] + u[2] * p[i][2])
            + u[i] * (mass_sq - m[4])
        )
        for i in range(3)
    ]


def cell_state(state, moments, rate_class, wall):
    density = state[0]
    inv = 1.0 / density
    u = [state[i] * inv for i in (1, 2, 3)]
    temperature = (2.0 * state[4] * inv - (u[0] * u[0] + u[1] * u[1] + u[2] * u[2])) * (1.0 / 3.0)
    heat = heat_flux(moments)
    frequency = 0.5 * jnp.exp2(rate_class.astype(F32))
    power = jnp.exp((1.0 - 0.81) * jnp.log(temperature))
    keep = jnp.exp(-STEP * frequency * density * power)
    inv_t = 1.0 / temperature
    rate = 1.0 - keep
    skew = ((1.0 - 2.0 / 3.0) / 5.0) * inv * inv_t * inv_t
    amplitude = rate * density * inv_t * lax.rsqrt(temperature)
    solid = wall > 0
    keep = jnp.where(solid, 0.0, keep)
    amplitude = jnp.where(solid, density, amplitude)
    inv_t = jnp.where(solid, 1.0, inv_t)
    u = [jnp.where(solid, 0.0, c) for c in u]
    heat = [jnp.where(solid, 0.0, skew * h) for h in heat]
    return keep, amplitude, inv_t, u, heat


def apply_added(sy, sz, cell):
    _, amplitude, inv_t, u, heat = cell
    dy, dz = sy - u[1], sz - u[2]
    square = (dy * dy + dz * dz) * inv_t
    return amplitude * jnp.exp(-0.5 * square), square - 5.0, dy * heat[1] + dz * heat[2]


def profile_x(cell, profile):
    _, _, inv_t, u, heat = cell
    for ix in range(VX):
        dx = SPEED_X[ix] - u[0]
        square = dx * dx * inv_t
        profile[0, ix] = jnp.exp(-0.5 * square)
        profile[1, ix] = square
        profile[2, ix] = dx * heat[0]


def line_sums(speeds, u, inv_t, top):
    out = [None] * (top + 1)
    for s in speeds:
        d = s - u
        term = jnp.exp(-0.5 * (d * d * inv_t))
        for b in range(top + 1):
            term = term if b == 0 else d * term
            out[b] = term if out[b] is None else out[b] + term
    return out


def mixed(raw, u, top):
    columns = [raw]
    for _ in range(top):
        last = columns[-1]
        columns.append([u * last[b] + last[b + 1] for b in range(len(last) - 1)])
    return [[column[b] for column in columns] for b in range(4)]


def added_moments(cell):
    _, amplitude, inv_t, u, heat = cell
    scale = amplitude * QUAD
    half = VX // 2
    x_up = mixed(line_sums(SPEED_X[half:], u[0], inv_t, 7), u[0], 4)
    x_dn = mixed(line_sums(SPEED_X[:half], u[0], inv_t, 7), u[0], 4)
    y_up = mixed(line_sums(SPEED_Y[half:], u[1], inv_t, 7), u[1], 4)
    y_dn = mixed(line_sums(SPEED_Y[:half], u[1], inv_t, 7), u[1], 4)
    z_all = mixed([scale * z for z in line_sums(SPEED_Z, u[2], inv_t, 6)], u[2], 3)
    x_all = [[p + q for p, q in zip(r, s)] for r, s in zip(x_up, x_dn)]
    y_all = [[p + q for p, q in zip(r, s)] for r, s in zip(y_up, y_dn)]
    gx, gy, gz = heat
    hx, hy, hz = gx * inv_t, gy * inv_t, gz * inv_t

    def whole(xs, ys):
        plane = {}

        def at(a, b):
            if (a, b) not in plane:
                x = [xs[i][a] for i in range(4)]
                y = [ys[i][b] for i in range(4)]
                x0y0 = x[0] * y[0]
                x1y0, x0y1 = x[1] * y[0], x[0] * y[1]
                x2y0, x0y2 = x[2] * y[0], x[0] * y[2]
                p0 = (
                    x0y0
                    + hx * (x[3] * y[0] + x[1] * y[2])
                    + hy * (x[2] * y[1] + x[0] * y[3])
                    - 5.0 * (gx * x1y0 + gy * x0y1)
                )
                p1 = hz * (x2y0 + x0y2) - 5.0 * gz * x0y0
                p2 = hx * x1y0 + hy * x0y1
                p3 = hz * x0y0
                plane[a, b] = (p0, p1, p2, p3)
            return plane[a, b]

        out = []
        for monos in MOMENTS:
            total = None
            for a, b, c in monos:
                p = at(a, b)
                term = (
                    p[0] * z_all[0][c] + p[1] * z_all[1][c] + p[2] * z_all[2][c] + p[3] * z_all[3][c]
                )
                total = term if total is None else total + term
            out.append(total)
        return out

    def weighted(table, factor):
        return [[factor * v for v in line[1:5]] for line in table]

    return (
        whole(x_all, y_all),
        whole(weighted(x_up, STEP), y_all),
        whole(weighted(x_dn, -STEP), y_all),
        whole(x_all, weighted(y_up, STEP)),
        whole(x_all, weighted(y_dn, -STEP)),
    )


def flat(cell):
    keep, amplitude, inv_t, u, heat = cell
    return [keep, amplitude, inv_t, *u, *heat]


def cell_of(v):
    return v[0], v[1], v[2], v[3:6], v[6:9]


def keep_out(cell, ref):
    for i, v in enumerate(flat(cell)):
        ref[i] = v


def first_kernel(
    q_ref, prev_ref, next_ref, class_ref, wall_ref, last_ref, first_ref, inner_last_ref, inner_first_ref,
    m_ref, add_ref, to_next_ref, to_prev_ref, cell_ref,
):
    block, iz = place()
    row = rows_of()
    shift = jnp.where(block >= 2, 1, 127)

    def line(ref, first, at):
        return ref[at[0] - first, at[1] : at[1] + 1, :]

    def whole_set(i):
        above, below = line(prev_ref, 0, row_up(i)), line(next_ref, 6, row_down(i))
        return q_ref[slot_of(i)] + jnp.where(row == 0, above, jnp.where(row == 7, below, 0.0))

    sets = [whole_set(i) for i in range(SETS)]
    scale = [1.0, 1.0, 1.0, 1.0, 0.5]
    state = []
    for k in range(5):
        far = jnp.where(row < 4, next_ref[1 + k], prev_ref[FIRST_SET + k])
        up, down = line(q_ref, 0, row_up(k)), line(q_ref, 0, row_down(k))
        far = far + jnp.where(row == 0, up, jnp.where(row == 7, down, 0.0))
        state.append(diffuse(scale[k] * sets[k], scale[k] * far, row))
    cell = cell_state(state, sets[:13], class_ref[...], wall_ref[...])
    keep = cell[0]
    keep_out(cell, cell_ref)
    sz = local_z(iz)

    for r, base_x, outer, inner, out in (
        (7, 0.0, last_ref, inner_last_ref, to_next_ref),
        (0, -EDGE, first_ref, inner_first_ref, to_prev_ref),
    ):
        line_cell = cell_of([jnp.broadcast_to(v[r : r + 1, :], (8, 128)) for v in flat(cell)])
        parts = []
        for j in range(2):
            sx = (row.astype(F32) + 0.5) * HX + (base_x + 8 * HX * j)
            dx = sx - line_cell[3][0]
            square = dx * dx * line_cell[2]
            parts.append(
                (STEP * jnp.abs(sx), jnp.exp(-0.5 * square), square, dx * line_cell[4][0])
            )

        def edge_y(iy, carry, line_cell=line_cell, parts=parts, outer=outer, inner=inner, out=out):
            sy = local_y(block, iy)
            courant_y = STEP * jnp.abs(sy)
            base, square, flux = apply_added(sy, sz, line_cell)
            for j, (courant_x, bell, square_x, flux_x) in enumerate(parts):
                value = outer[2 * iy + j]
                value = (
                    ((1.0 - courant_x) - courant_y) * value
                    + courant_x * inner[2 * iy + j]
                    + courant_y * pltpu.roll(value, shift, 1)
                )
                added = (base * bell) * (1.0 + (flux + flux_x) * (square + square_x))
                out[6 + 2 * iy + j] = line_cell[0] * value + added
            return carry

        lax.fori_loop(0, 8, edge_y, 0, unroll=True)

    g_all, g_xu, g_xd, g_yu, g_yd = added_moments(cell)
    part = 0.5 * STEP * keep
    for k, monos in enumerate(MOMENTS):
        sx_k, ax_k = sets[AT[key_of(times(monos, 0))]], sets[ABS_X + k]
        sy_k, ay_k = sets[AT[key_of(times(monos, 1))]], sets[ABS_Y + k]
        x_up = part * (ax_k + sx_k) + g_xu[k]
        x_dn = part * (ax_k - sx_k) + g_xd[k]
        y_up = part * (ay_k + sy_k) + g_yu[k]
        y_dn = part * (ay_k - sy_k) + g_yd[k]
        from_up, from_dn = pltpu.roll(x_up, 1, 0), pltpu.roll(x_dn, 7, 0)
        total = (
            (keep * sets[k] + g_all[k] - x_up - x_dn - y_up - y_dn)
            + jnp.where(row == 0, 0.0, from_up)
            + jnp.where(row == 7, 0.0, from_dn)
            + pltpu.roll(y_up, 1, 1)
            + pltpu.roll(y_dn, 127, 1)
        )
        m_ref[k] = total
        if k < 5:
            add_ref[k] = jnp.where(row == 0, from_up, jnp.where(row == 7, from_dn, 0.0))
            to_next_ref[k] = jnp.where(row == 0, from_up, total)
            to_prev_ref[k] = jnp.where(row == 7, from_dn, total)
        else:
            to_next_ref[5, k - 5 : k - 4, :] = x_up[7:8, :]
            to_prev_ref[5, k - 5 : k - 4, :] = x_dn[0:1, :]


def field_kernel(cell_ref, f_ref, before_ref, after_ref, t_ref, profile):
    block, iz = place()
    row = rows_of()
    shift = jnp.where(block >= 2, 1, 127)
    cell = cell_of([cell_ref[i] for i in range(9)])
    keep = cell[0]
    profile_x(cell, profile)
    sz = local_z(iz)

    def over_y(iy, carry):
        sy = local_y(block, iy)
        courant_y = STEP * jnp.abs(sy)
        base, square, flux = apply_added(sy, sz, cell)
        for ix in range(VX):
            k = ix % 16
            edge = (before_ref if SPEED_X[ix] > 0 else after_ref)[
                12 + 2 * iy + k // 8, k % 8 : k % 8 + 1, :
            ]
            value = moved(f_ref[iy * 32 + ix], ix, courant_y, shift, row, edge, edge)
            added = (base * profile[0, ix]) * (
                1.0 + (flux + profile[2, ix]) * (square + profile[1, ix])
            )
            value = keep * value + added
            t_ref[iy * 32 + ix] = moved(value, ix, courant_y, shift, row, 0.0, 0.0)
        return carry

    lax.fori_loop(0, 8, over_y, 0)


def second_kernel(
    m_ref, add_ref, prev_ref, next_ref, class_ref, wall_ref, t_ref,
    out_ref, state_ref, profile, cell_ref,
):
    block, iz = place()
    row = rows_of()
    step = pl.program_id(0)

    @pl.when(step == 0)
    def _():
        moments = []
        for k in range(13):
            if k < 5:
                before, after = prev_ref[k], next_ref[k]
            else:
                before, after = prev_ref[5, k - 5 : k - 4, :], next_ref[5, k - 5 : k - 4, :]
            moments.append(
                m_ref[k] + jnp.where(row == 0, before, jnp.where(row == 7, after, 0.0))
            )
        scale = [1.0, 1.0, 1.0, 1.0, 0.5]
        state = []
        for k in range(5):
            far = jnp.where(row < 4, next_ref[k], prev_ref[k]) + add_ref[k]
            state.append(diffuse(scale[k] * moments[k], scale[k] * far, row))
            state_ref[k] = state[k]
        cell = cell_state(state, moments, class_ref[...], wall_ref[...])
        profile_x(cell, profile)
        keep_out(cell, cell_ref)

    cell = cell_of([cell_ref[i] for i in range(9)])
    keep = cell[0]
    sz = local_z(iz)

    def over_y(iy, carry):
        sy = local_y(block, iy)
        base, square, flux = apply_added(sy, sz, cell)
        for ix in range(VX):
            k = ix % 16
            edge = (prev_ref if SPEED_X[ix] > 0 else next_ref)[
                6 + 2 * iy + k // 8, k % 8 : k % 8 + 1, :
            ]
            courant_x = STEP * abs(SPEED_X[ix])
            here = row == (0 if SPEED_X[ix] > 0 else 7)
            value = t_ref[iy * 32 + ix] + jnp.where(here, courant_x * edge, 0.0)
            added = (base * profile[0, ix]) * (
                1.0 + (flux + profile[2, ix]) * (square + profile[1, ix])
            )
            out_ref[(iy - 4 * step) * 32 + ix] = keep * value + added
        return carry

    lax.fori_loop(4 * step, 4 * (step + 1), over_y, 0)


def kernel_call(body, outs, scratch, limit=32, **kw):
    return pl.pallas_call(
        body,
        out_shape=[jax.ShapeDtypeStruct(s, F32) for s in outs],
        scratch_shapes=[pltpu.VMEM(s, F32) if isinstance(s, tuple) else s for s in scratch],
        **kw,
        compiler_params=pltpu.CompilerParams(vmem_limit_bytes=limit * 1024 * 1024),
    )


def to_both(up_value, down_value):
    size = lax.axis_size("space")
    up = [(i, (i + 1) % size) for i in range(size)]
    down = [(j, i) for i, j in up]
    return lax.ppermute(up_value, "space", up), lax.ppermute(down_value, "space", down)


NEAR = [
    [(4 * b + k) * 4 + y for k in order for y in (2, 3, 1, 0)]
    for b, order in enumerate(((1, 0, 2, 3), (2, 3, 1, 0), (1, 0, 2, 3), (1, 0, 2, 3)))
]
FAR = [[NEAR[b][p] for b in (2, 0, 1, 3)] for p in range(16)]


def all_sum(part):
    piece = part.reshape(16, SLOTS // 2, 128)
    piece = lax.all_to_all(piece, "vel", 0, 0, tiled=True, axis_index_groups=NEAR)
    mine = jnp.sum(piece, 0)
    piece = jnp.broadcast_to(mine[None], (4,) + mine.shape)
    piece = lax.all_to_all(piece, "vel", 0, 0, tiled=True, axis_index_groups=FAR)
    mine = jnp.sum(piece, 0)
    piece = jnp.broadcast_to(mine[None], (16,) + mine.shape)
    piece = lax.all_to_all(piece, "vel", 0, 0, tiled=True, axis_index_groups=NEAR)
    return piece.reshape(SLOTS, 8, 128)


def per_device(distribution, rate_class, wall):
    block, edges, small = (256, 8, 128), (16, 8, 128), (22, 8, 128)
    part, last, first, inner_last, inner_first = kernel_call(
        moments_kernel,
        [(SLOTS, 8, 128)] + [edges] * 4,
        [block, (25, 8, 128), (2, 15, 8, 128), pltpu.SemaphoreType.DMA((4,))],
        limit=53,
        in_specs=[pl.BlockSpec(memory_space=pltpu.HBM)],
    )(distribution)
    sums = all_sum(part)
    prev_sums, next_sums = to_both(
        jnp.concatenate([sums[:12], last]), jnp.concatenate([sums[6:18], first])
    )
    moments, extra, to_next, to_prev, cell = kernel_call(
        first_kernel, [(13, 8, 128), (5, 8, 128), small, small, (9, 8, 128)], []
    )(sums, prev_sums, next_sums, rate_class, wall, last, first, inner_last, inner_first)
    prev, following = to_both(to_next, to_prev)
    (moved_field,) = kernel_call(field_kernel, [block], [(3, 32, 8, 128)])(
        cell, distribution, prev_sums, next_sums
    )
    whole = pl.BlockSpec(memory_space=pltpu.VMEM)
    field, state = kernel_call(
        second_kernel,
        [block, (5, 8, 128)],
        [(3, 32, 8, 128), (9, 8, 128)],
        grid=(2,),
        in_specs=[whole] * 7,
        out_specs=[
            pl.BlockSpec((128, 8, 128), lambda i: (i, 0, 0)),
            pl.BlockSpec((5, 8, 128), lambda i: (0, 0, 0)),
        ],
    )(
        moments, extra, prev, following, rate_class, wall, moved_field
    )
    return field, state


def solution(mesh):
    return jax.shard_map(
        per_device,
        mesh=mesh,
        in_specs=(P("vel", "space", None), P("space", None), P("space", None)),
        out_specs=(P("vel", "space", None), P(None, "space", None)),
        check_vma=False,
    )
```

profile of v0, /device:TPU:7, one launch (start us, length us, event | category | flops | bytes accessed | tf_op | source)
XLA Modules:
  0.0 63.4 jit_solution(55700238337589406)
XLA Ops:
  0.6 2.1 %shard_map.50 = (f32[64,8,128]{2,1,0:T(8,128)S(1)}, f32[16,8,128]{2,1,0:T(8,128)S(1)}, f32[16,8,128]{2,1,0:T(8,128)S(1)}, f32[16,8,128]{2,1,0:T(8,128)S(1)}, f32[16,8,128]{2,1,0:T(8,128)S(1)}) custom-call(f32[256,8,128]{2,1,0:T(8,128)} %f_ref.1), custom_call_target="tpu_custom_call" | custom-call | tf_op jit(solution)/shard_map/pallas_call | solution.py:575
  2.8 15.4 %all_to_all.15 = f32[16,32,128]{2,1,0:T(8,128)S(1)} all-to-all(f32[16,32,128]{2,1,0:T(8,128)S(1)} %bitcast.5), channel_id=1, replica_groups={{48,56,40,32,16,24,8,0,80,88,72,64,112,120,104,96},{208,216,200,192,240..., dimensions={0} | all-to-all | bytes 524288 | tf_op jit(solution)/shard_map/all_to_all | solution.py:563
  18.2 16.1 %all_to_all.16 = f32[4,32,128]{2,1,0:T(8,128)S(1)} all-to-all(f32[4,32,128]{2,1,0:T(8,128)S(1)} %broadcast_in_dim.4), channel_id=1, replica_groups={{304,48,208,432},{312,56,216,440},{296,40,200,424},{288,32,192,416},{27..., dimensions={0} | all-to-all | bytes 131072 | tf_op jit(solution)/shard_map/all_to_all | solution.py:566
  34.3 0.0 copy-start
  34.3 10.5 %all_to_all.17 = f32[16,32,128]{2,1,0:T(8,128)S(1)} all-to-all(f32[16,32,128]{2,1,0:T(8,128)S(1)} %broadcast_in_dim.5), channel_id=1, replica_groups={{48,56,40,32,16,24,8,0,80,88,72,64,112,120,104,96},{208,216,200,192,240..., dimensions={0} | all-to-all | bytes 524288 | tf_op jit(solution)/shard_map/all_to_all | solution.py:569
  44.9 4.9 %collective-permute-start.1 = (f32[28,8,128]{2,1,0:T(8,128)S(1)}, f32[28,8,128]{2,1,0:T(8,128)S(1)}, u32[]{:S(2)}, u32[]{:S(2)}) collective-permute-start(f32[28,8,128]{2,1,0:T(8,128)S(1)} %pad_maximum_fusion.1), channel_id=1, source_target_pairs={{1,0},{2,1},{3,2},{4,3},{5,4},{6,5},{7,6},{0,7},{9,8},{10,9},{11,1... | collective-permute-start | bytes 344072 | tf_op jit(solution)/shard_map/ppermute | solution.py:551
  49.8 0.0 copy-start.1
  49.8 0.0 copy-start.2
  49.9 0.1 collective-permute-start
  50.0 2.4 %collective-permute-done.1.next_ref.after_ref = f32[28,8,128]{2,1,0:T(8,128)S(1)} collective-permute-done((f32[28,8,128]{2,1,0:T(8,128)S(1)}, f32[28,8,128]{2,1,0:T(8,128)S(1)}, u32[]{:S(2)}, u32[]{:S(2)}) %collective-permute-start.1) | collective-permute-done | bytes 114720 | tf_op jit(solution)/shard_map/ppermute | solution.py:551
  52.4 0.0 collective-permute-done.prev_ref.before_ref
  52.4 0.0 copy-done.1
  52.4 0.0 copy-done.2
  52.4 1.1 %shard_map.51 = (f32[13,8,128]{2,1,0:T(8,128)S(1)}, f32[5,8,128]{2,1,0:T(8,128)S(1)}, f32[22,8,128]{2,1,0:T(8,128)S(1)}, f32[22,8,128]{2,1,0:T(8,128)S(1)}, f32[9,8,128]{2,1,0:T(8,128)S(1)}) custom-call(f32[64,8,128]{2,1,0:T(8,128)S(1)} %bitcast.4, f32[28,8,128]{2,1,0:T(8,128)S(1)} %collective-permute-done.prev_ref.before_ref, ...), custom_call_target="tpu_custom_call" | custom-call | tf_op jit(solution)/shard_map/pallas_call | solution.py:586
  53.5 3.0 %collective-permute-start.2 = (f32[22,8,128]{2,1,0:T(8,128)S(1)}, f32[22,8,128]{2,1,0:T(8,128)S(1)}, u32[]{:S(2)}, u32[]{:S(2)}) collective-permute-start(f32[22,8,128]{2,1,0:T(8,128)S(1)} %get-tuple-element.19), channel_id=1, source_target_pairs={{0,1},{1,2},{2,3},{3,4},{4,5},{5,6},{6,7},{7,0},{8,9},{9,10},{10,1... | collective-permute-start | bytes 270344 | tf_op jit(solution)/shard_map/ppermute | solution.py:551
  56.5 0.0 collective-permute-start.3
  56.5 0.0 copy-done
  56.5 1.5 %shard_map.52.t_ref = f32[256,8,128]{2,1,0:T(8,128)S(1)} custom-call(f32[9,8,128]{2,1,0:T(8,128)S(1)} %get-tuple-element.21.cell_ref, f32[256,8,128]{2,1,0:T(8,128)S(1)} %copy-done, f32[28,8,128]{2,1,0:T(8,128)S(1)} %collective-permute-done.prev_ref.before_ref, f32[28,8,128]{2,1,0:T(8,128)S(1)} %collective-permute-done.1.next_ref.after_ref), custom_call_target="tpu_custom_call" | custom-call | tf_op jit(solution)/shard_map/pallas_call | solution.py:590
  58.0 0.1 collective-permute-done.2.prev_ref
  58.1 3.6 %collective-permute-done.3.next_ref = f32[22,8,128]{2,1,0:T(8,128)S(1)} collective-permute-done((f32[22,8,128]{2,1,0:T(8,128)S(1)}, f32[22,8,128]{2,1,0:T(8,128)S(1)}, u32[]{:S(2)}, u32[]{:S(2)}) %collective-permute-start.3) | collective-permute-done | bytes 90144 | tf_op jit(solution)/shard_map/ppermute | solution.py:551
  61.7 1.7 %shard_map.53 = (f32[256,8,128]{2,1,0:T(8,128)}, f32[5,8,128]{2,1,0:T(8,128)}) custom-call(f32[13,8,128]{2,1,0:T(8,128)S(1)} %get-tuple-element.17.m_ref, f32[5,8,128]{2,1,0:T(8,128)S(1)} %get-tuple-element.18.add_ref, f32[22,8,128]{2,1,0:T(8,128)S(1)} %collective-permute-done.2.prev_ref, f32[22,8,128]{2,1,0:T(8,128)S(1)} %collective-permute-done.3.next_ref, ...), custom_call_target="tpu_custom_call" | custom-call | tf_op jit(solution)/shard_map/pallas_call | solution.py:594
  (8 shorter events, 0.1 us)
Async XLA Ops:
  34.3 22.2 %copy-start = (f32[256,8,128]{2,1,0:T(8,128)S(1)}, f32[256,8,128]{2,1,0:T(8,128)}, u32[]{:S(2)}) copy-start(f32[256,8,128]{2,1,0:T(8,128)} %f_ref.1) | copy-start | bytes 3145732
  44.9 7.5 %collective-permute-start.1 = (f32[28,8,128]{2,1,0:T(8,128)S(1)}, f32[28,8,128]{2,1,0:T(8,128)S(1)}, u32[]{:S(2)}, u32[]{:S(2)}) collective-permute-start(f32[28,8,128]{2,1,0:T(8,128)S(1)} %pad_maximum_fusion.1), channel_id=1, source_target_pairs={{1,0},{2,1},{3,2},{4,3},{5,4},{6,5},{7,6},{0,7},{9,8},{10,9},{11,1... | collective-permute-start | bytes 344072 | tf_op jit(solution)/shard_map/ppermute | solution.py:551
  49.8 2.6 %copy-start.1 = (s32[8,128]{1,0:T(8,128)S(1)}, s32[8,128]{1,0:T(8,128)}, u32[]{:S(2)}) copy-start(s32[8,128]{1,0:T(8,128)} %class_ref.3) | copy-start | bytes 12292
  49.8 2.6 %copy-start.2 = (s32[8,128]{1,0:T(8,128)S(1)}, s32[8,128]{1,0:T(8,128)}, u32[]{:S(2)}) copy-start(s32[8,128]{1,0:T(8,128)} %wall_ref.3) | copy-start | bytes 12292
  49.9 2.5 %collective-permute-start = (f32[28,8,128]{2,1,0:T(8,128)S(1)}, f32[28,8,128]{2,1,0:T(8,128)S(1)}, u32[]{:S(2)}, u32[]{:S(2)}) collective-permute-start(f32[28,8,128]{2,1,0:T(8,128)S(1)} %pad_maximum_fusion), channel_id=1, source_target_pairs={{0,1},{1,2},{2,3},{3,4},{4,5},{5,6},{6,7},{7,0},{8,9},{9,10},{10,1... | collective-permute-start | bytes 344072 | tf_op jit(solution)/shard_map/ppermute | solution.py:551
  53.5 4.6 %collective-permute-start.2 = (f32[22,8,128]{2,1,0:T(8,128)S(1)}, f32[22,8,128]{2,1,0:T(8,128)S(1)}, u32[]{:S(2)}, u32[]{:S(2)}) collective-permute-start(f32[22,8,128]{2,1,0:T(8,128)S(1)} %get-tuple-element.19), channel_id=1, source_target_pairs={{0,1},{1,2},{2,3},{3,4},{4,5},{5,6},{6,7},{7,0},{8,9},{9,10},{10,1... | collective-permute-start | bytes 270344 | tf_op jit(solution)/shard_map/ppermute | solution.py:551
  56.5 5.2 %collective-permute-start.3 = (f32[22,8,128]{2,1,0:T(8,128)S(1)}, f32[22,8,128]{2,1,0:T(8,128)S(1)}, u32[]{:S(2)}, u32[]{:S(2)}) collective-permute-start(f32[22,8,128]{2,1,0:T(8,128)S(1)} %get-tuple-element.20), channel_id=1, source_target_pairs={{1,0},{2,1},{3,2},{4,3},{5,4},{6,5},{7,6},{0,7},{9,8},{10,9},{11,1... | collective-permute-start | bytes 270344 | tf_op jit(solution)/shard_map/ppermute | solution.py:551
where the time goes:
time: 63.6 us; the launch traced here: 63.4 us
  blocking collectives  42 us (66%)
  starting transfers between devices  8.11 us (13%)
  Pallas kernels  6.4 us (10%)
  waiting for transfers between devices  6.08 us (10%)
  between operations  0.7 us (1%)
    all_to_all x2, blocking collectives, all_sum(): lax.all_to_all(piece, 'vel', 0, 0, tiled=True, axis_index_groups=NEAR)  25.9 us
    all_to_all x1, blocking collectives, all_sum(): lax.all_to_all(piece, 'vel', 0, 0, tiled=True, axis_index_groups=FAR)  16.1 us
    ppermute x2, waiting for transfers between devices, to_both(): lax.ppermute(down_value, 'space', down)  6 us
    ppermute x2, starting transfers between devices, to_both(): lax.ppermute(down_value, 'space', down)  4.95 us
    ppermute x2, starting transfers between devices, to_both(): lax.ppermute(up_value, 'space', up)  3.16 us
    pallas_call x1, Pallas kernels, per_device(): kernel_call(moments_kernel, [(SLOTS, 8, 128)] + [edges] * 4, [block, (25,...  2.13 us
    pallas_call x1, Pallas kernels, per_device(): kernel_call(second_kernel, [block, (5, 8, 128)], [(3, 32, 8, 128), (9, 8,...  1.73 us
    pallas_call x1, Pallas kernels, per_device(): kernel_call(field_kernel, [block], [(3, 32, 8, 128)])  1.47 us
  transfers between devices with their start and end apart: 4, of which 3 were waited for; matrix products, arithmetic and copies ran while one was open for 0% of the time, Pallas kernels for 2%

commit v1 on v0

--- a/solution.py
+++ b/solution.py
@@ -1,3 +1,5 @@
+import math
+
 import jax
 import jax.numpy as jnp
 import numpy as np
@@ -195,24 +197,32 @@
 
 
 def diffuse(own_source, far_source, row):
-    own, far = own_source, far_source
-    for _ in range(SWEEPS):
+    weight = [0.2 ** (m + 1) for m in range(SWEEPS)] + [0.2**SWEEPS]
+
+    def along(x):
+        r = [None] + [pltpu.roll(x, d, 1) + pltpu.roll(x, 128 - d, 1) for d in (1, 2, 3, 4)]
+        h = [x, r[1], r[2] + 2.0 * x, r[3] + 3.0 * r[1], r[4] + 4.0 * r[2] + 6.0 * x]
+        return [
+            added_up((weight[i + j] * math.comb(i + j, i)) * h[j] for j in range(5 - i))
+            for i in range(5)
+        ]
+
+    own_terms, far_terms = along(own_source), along(far_source)
+    own, far = own_terms[4], far_terms[4]
+    for i in (3, 2, 1, 0):
         own_down, far_down = pltpu.roll(own, 1, 0), pltpu.roll(far, 1, 0)
         own_up, far_up = pltpu.roll(own, 7, 0), pltpu.roll(far, 7, 0)
-        new_own = (
-            jnp.where(row == 0, far_down, own_down)
+        own = (
+            own_terms[i]
+            + jnp.where(row == 0, far_down, own_down)
             + jnp.where(row == 7, far_up, own_up)
-            + pltpu.roll(own, 1, 1)
-            + pltpu.roll(own, 127, 1)
         )
-        new_far = (
-            jnp.where(row == 0, own_down, far_down)
-            + jnp.where(row == 7, own_up, far_up)
-            + pltpu.roll(far, 1, 1)
-            + pltpu.roll(far, 127, 1)
-        )
-        own = (own_source + new_own) * 0.2
-        far = (far_source + new_far) * 0.2
+        if i:
+            far = (
+                far_terms[i]
+                + jnp.where(row == 0, own_down, far_down)
+                + jnp.where(row == 7, own_up, far_up)
+            )
     return own
 
 

time: 63.6 us -> 63.3 us (level)
  no operation moved by 1% of the time
where the time goes in v1:
time: 63.3 us; the launch traced here: 63.1 us
  blocking collectives  42 us (66%)
  starting transfers between devices  8.11 us (13%)
  Pallas kernels  6.11 us (10%)
  waiting for transfers between devices  6.08 us (10%)
  between operations  0.7 us (1%)
    all_to_all x2, blocking collectives, all_sum(): lax.all_to_all(piece, 'vel', 0, 0, tiled=True, axis_index_groups=NEAR)  25.9 us
    all_to_all x1, blocking collectives, all_sum(): lax.all_to_all(piece, 'vel', 0, 0, tiled=True, axis_index_groups=FAR)  16.1 us
    ppermute x2, waiting for transfers between devices, to_both(): lax.ppermute(down_value, 'space', down)  6 us
    ppermute x2, starting transfers between devices, to_both(): lax.ppermute(down_value, 'space', down)  4.95 us
    ppermute x2, starting transfers between devices, to_both(): lax.ppermute(up_value, 'space', up)  3.16 us
    pallas_call x1, Pallas kernels, per_device(): kernel_call(moments_kernel, [(SLOTS, 8, 128)] + [edges] * 4, [block, (25,...  2.13 us
    pallas_call x1, Pallas kernels, per_device(): kernel_call(second_kernel, [block, (5, 8, 128)], [(3, 32, 8, 128), (9, 8,...  1.59 us
    pallas_call x1, Pallas kernels, per_device(): kernel_call(field_kernel, [block], [(3, 32, 8, 128)])  1.47 us
  transfers between devices with their start and end apart: 4, of which 3 were waited for; matrix products, arithmetic and copies ran while one was open for 0% of the time, Pallas kernels for 2%

profile of v1, /device:TPU:7, one launch (start us, length us, event | category | flops | bytes accessed | tf_op | source)
XLA Modules:
  0.0 63.1 jit_solution(14237015419218962500)
XLA Ops:
  0.6 2.1 %shard_map.50 = (f32[64,8,128]{2,1,0:T(8,128)S(1)}, f32[16,8,128]{2,1,0:T(8,128)S(1)}, f32[16,8,128]{2,1,0:T(8,128)S(1)}, f32[16,8,128]{2,1,0:T(8,128)S(1)}, f32[16,8,128]{2,1,0:T(8,128)S(1)}) custom-call(f32[256,8,128]{2,1,0:T(8,128)} %f_ref.1), custom_call_target="tpu_custom_call" | custom-call | tf_op jit(solution)/shard_map/pallas_call | solution.py:585
  2.8 15.4 %all_to_all.15 = f32[16,32,128]{2,1,0:T(8,128)S(1)} all-to-all(f32[16,32,128]{2,1,0:T(8,128)S(1)} %bitcast.5), channel_id=1, replica_groups={{48,56,40,32,16,24,8,0,80,88,72,64,112,120,104,96},{208,216,200,192,240..., dimensions={0} | all-to-all | bytes 524288 | tf_op jit(solution)/shard_map/all_to_all | solution.py:573
  18.2 16.1 %all_to_all.16 = f32[4,32,128]{2,1,0:T(8,128)S(1)} all-to-all(f32[4,32,128]{2,1,0:T(8,128)S(1)} %broadcast_in_dim.4), channel_id=1, replica_groups={{304,48,208,432},{312,56,216,440},{296,40,200,424},{288,32,192,416},{27..., dimensions={0} | all-to-all | bytes 131072 | tf_op jit(solution)/shard_map/all_to_all | solution.py:576
  34.3 0.0 copy-start
  34.3 10.5 %all_to_all.17 = f32[16,32,128]{2,1,0:T(8,128)S(1)} all-to-all(f32[16,32,128]{2,1,0:T(8,128)S(1)} %broadcast_in_dim.5), channel_id=1, replica_groups={{48,56,40,32,16,24,8,0,80,88,72,64,112,120,104,96},{208,216,200,192,240..., dimensions={0} | all-to-all | bytes 524288 | tf_op jit(solution)/shard_map/all_to_all | solution.py:579
  44.9 4.9 %collective-permute-start.1 = (f32[28,8,128]{2,1,0:T(8,128)S(1)}, f32[28,8,128]{2,1,0:T(8,128)S(1)}, u32[]{:S(2)}, u32[]{:S(2)}) collective-permute-start(f32[28,8,128]{2,1,0:T(8,128)S(1)} %pad_maximum_fusion.1), channel_id=1, source_target_pairs={{1,0},{2,1},{3,2},{4,3},{5,4},{6,5},{7,6},{0,7},{9,8},{10,9},{11,1... | collective-permute-start | bytes 344072 | tf_op jit(solution)/shard_map/ppermute | solution.py:561
  49.8 0.0 copy-start.1
  49.8 0.0 copy-start.2
  49.9 0.1 collective-permute-start
  50.0 2.4 %collective-permute-done.1.next_ref.after_ref = f32[28,8,128]{2,1,0:T(8,128)S(1)} collective-permute-done((f32[28,8,128]{2,1,0:T(8,128)S(1)}, f32[28,8,128]{2,1,0:T(8,128)S(1)}, u32[]{:S(2)}, u32[]{:S(2)}) %collective-permute-start.1) | collective-permute-done | bytes 114720 | tf_op jit(solution)/shard_map/ppermute | solution.py:561
  52.4 0.0 collective-permute-done.prev_ref.before_ref
  52.4 0.0 copy-done.1
  52.4 0.0 copy-done.2
  52.4 0.9 %shard_map.51 = (f32[13,8,128]{2,1,0:T(8,128)S(1)}, f32[5,8,128]{2,1,0:T(8,128)S(1)}, f32[22,8,128]{2,1,0:T(8,128)S(1)}, f32[22,8,128]{2,1,0:T(8,128)S(1)}, f32[9,8,128]{2,1,0:T(8,128)S(1)}) custom-call(f32[64,8,128]{2,1,0:T(8,128)S(1)} %bitcast.4, f32[28,8,128]{2,1,0:T(8,128)S(1)} %collective-permute-done.prev_ref.before_ref, ...), custom_call_target="tpu_custom_call" | custom-call | tf_op jit(solution)/shard_map/pallas_call | solution.py:596
  53.3 3.0 %collective-permute-start.2 = (f32[22,8,128]{2,1,0:T(8,128)S(1)}, f32[22,8,128]{2,1,0:T(8,128)S(1)}, u32[]{:S(2)}, u32[]{:S(2)}) collective-permute-start(f32[22,8,128]{2,1,0:T(8,128)S(1)} %get-tuple-element.19), channel_id=1, source_target_pairs={{0,1},{1,2},{2,3},{3,4},{4,5},{5,6},{6,7},{7,0},{8,9},{9,10},{10,1... | collective-permute-start | bytes 270344 | tf_op jit(solution)/shard_map/ppermute | solution.py:561
  56.4 0.0 collective-permute-start.3
  56.4 0.0 copy-done
  56.4 1.5 %shard_map.52.t_ref = f32[256,8,128]{2,1,0:T(8,128)S(1)} custom-call(f32[9,8,128]{2,1,0:T(8,128)S(1)} %get-tuple-element.21.cell_ref, f32[256,8,128]{2,1,0:T(8,128)S(1)} %copy-done, f32[28,8,128]{2,1,0:T(8,128)S(1)} %collective-permute-done.prev_ref.before_ref, f32[28,8,128]{2,1,0:T(8,128)S(1)} %collective-permute-done.1.next_ref.after_ref), custom_call_target="tpu_custom_call" | custom-call | tf_op jit(solution)/shard_map/pallas_call | solution.py:600
  57.8 0.1 collective-permute-done.2.prev_ref
  57.9 3.6 %collective-permute-done.3.next_ref = f32[22,8,128]{2,1,0:T(8,128)S(1)} collective-permute-done((f32[22,8,128]{2,1,0:T(8,128)S(1)}, f32[22,8,128]{2,1,0:T(8,128)S(1)}, u32[]{:S(2)}, u32[]{:S(2)}) %collective-permute-start.3) | collective-permute-done | bytes 90144 | tf_op jit(solution)/shard_map/ppermute | solution.py:561
  61.5 1.6 %shard_map.53 = (f32[256,8,128]{2,1,0:T(8,128)}, f32[5,8,128]{2,1,0:T(8,128)}) custom-call(f32[13,8,128]{2,1,0:T(8,128)S(1)} %get-tuple-element.17.m_ref, f32[5,8,128]{2,1,0:T(8,128)S(1)} %get-tuple-element.18.add_ref, f32[22,8,128]{2,1,0:T(8,128)S(1)} %collective-permute-done.2.prev_ref, f32[22,8,128]{2,1,0:T(8,128)S(1)} %collective-permute-done.3.next_ref, ...), custom_call_target="tpu_custom_call" | custom-call | tf_op jit(solution)/shard_map/pallas_call | solution.py:604
  (8 shorter events, 0.1 us)
Async XLA Ops:
  34.3 22.0 %copy-start = (f32[256,8,128]{2,1,0:T(8,128)S(1)}, f32[256,8,128]{2,1,0:T(8,128)}, u32[]{:S(2)}) copy-start(f32[256,8,128]{2,1,0:T(8,128)} %f_ref.1) | copy-start | bytes 3145732
  44.9 7.5 %collective-permute-start.1 = (f32[28,8,128]{2,1,0:T(8,128)S(1)}, f32[28,8,128]{2,1,0:T(8,128)S(1)}, u32[]{:S(2)}, u32[]{:S(2)}) collective-permute-start(f32[28,8,128]{2,1,0:T(8,128)S(1)} %pad_maximum_fusion.1), channel_id=1, source_target_pairs={{1,0},{2,1},{3,2},{4,3},{5,4},{6,5},{7,6},{0,7},{9,8},{10,9},{11,1... | collective-permute-start | bytes 344072 | tf_op jit(solution)/shard_map/ppermute | solution.py:561
  49.8 2.6 %copy-start.1 = (s32[8,128]{1,0:T(8,128)S(1)}, s32[8,128]{1,0:T(8,128)}, u32[]{:S(2)}) copy-start(s32[8,128]{1,0:T(8,128)} %class_ref.3) | copy-start | bytes 12292
  49.8 2.6 %copy-start.2 = (s32[8,128]{1,0:T(8,128)S(1)}, s32[8,128]{1,0:T(8,128)}, u32[]{:S(2)}) copy-start(s32[8,128]{1,0:T(8,128)} %wall_ref.3) | copy-start | bytes 12292
  49.9 2.5 %collective-permute-start = (f32[28,8,128]{2,1,0:T(8,128)S(1)}, f32[28,8,128]{2,1,0:T(8,128)S(1)}, u32[]{:S(2)}, u32[]{:S(2)}) collective-permute-start(f32[28,8,128]{2,1,0:T(8,128)S(1)} %pad_maximum_fusion), channel_id=1, source_target_pairs={{0,1},{1,2},{2,3},{3,4},{4,5},{5,6},{6,7},{7,0},{8,9},{9,10},{10,1... | collective-permute-start | bytes 344072 | tf_op jit(solution)/shard_map/ppermute | solution.py:561
  53.3 4.6 %collective-permute-start.2 = (f32[22,8,128]{2,1,0:T(8,128)S(1)}, f32[22,8,128]{2,1,0:T(8,128)S(1)}, u32[]{:S(2)}, u32[]{:S(2)}) collective-permute-start(f32[22,8,128]{2,1,0:T(8,128)S(1)} %get-tuple-element.19), channel_id=1, source_target_pairs={{0,1},{1,2},{2,3},{3,4},{4,5},{5,6},{6,7},{7,0},{8,9},{9,10},{10,1... | collective-permute-start | bytes 270344 | tf_op jit(solution)/shard_map/ppermute | solution.py:561
  56.4 5.2 %collective-permute-start.3 = (f32[22,8,128]{2,1,0:T(8,128)S(1)}, f32[22,8,128]{2,1,0:T(8,128)S(1)}, u32[]{:S(2)}, u32[]{:S(2)}) collective-permute-start(f32[22,8,128]{2,1,0:T(8,128)S(1)} %get-tuple-element.20), channel_id=1, source_target_pairs={{1,0},{2,1},{3,2},{4,3},{5,4},{6,5},{7,6},{0,7},{9,8},{10,9},{11,1... | collective-permute-start | bytes 270344 | tf_op jit(solution)/shard_map/ppermute | solution.py:561
